TPU v7x, 256 devices: a whole 4x4x8 slice. The times are simulated.
256 devices in a mesh: ctx: 32 (over z, y_hi, core), tp: 8 (over x, y_lo).
Axes of the slice: x: 4, y: 4 (y_hi: 2, y_lo: 2; y = y_hi * 2 + y_lo), z: 8, core: 2. Of those that a mesh axis runs over, the one named last changes fastest.
Arguments:
- hidden_states: bfloat16 [8192, 4096], P('ctx', 'tp'), may hold values from -40 to 40
- w_query: bfloat16 [4096, 4096], P(None, 'tp'), may hold values from -0.25 to 0.25
- w_key: bfloat16 [4096, 1024], P(None, 'tp'), may hold values from -0.5 to 0.5
- w_value: bfloat16 [4096, 1024], P(None, 'tp'), may hold values from -0.09375 to 0.09375
- w_out: bfloat16 [4096, 4096], P('tp'), may hold values from -0.09375 to 0.09375
- span_order: int32 [64], replicated, may hold values from 0 to 63, each once
- lengths: int32 [4], replicated, may hold values from 1 to 4096, 8192 in all
Outputs:
- attention_out: bfloat16 [8192, 4096], P('ctx', 'tp')
Inputs may be any that keep to these rules, and one draw needn't show every extreme that they name: `span_order`: each value appears exactly once. `lengths`: they sum to 8192; the longest is exactly 4096.
All inputs are finite; a program needn't handle non-finite values.
Results may differ from a plain program's by a relative error of at most 0.02.
Values may be sent and summed in bfloat16 or wider, within the bound.
No kernel may reach another device: no remote copies, remote signals or barrier semaphores. Data moves between devices by JAX's collectives and lax.ppermute only.
A program may use at most 64 MiB of HBM per device.

v0:
```python
import math

import jax
import jax.numpy as jnp
from jax import lax
from jax.sharding import PartitionSpec as P

HEADS = 32
KV_HEADS = 8
HEAD_DIM = 128


ROPE_BASE = 500000.0
NEG_FILL = -1e30


def rotate_half(values, positions):
    head_dim = values.shape[-1]
    half_dim = head_dim // 2
    exponent = jnp.arange(half_dim, dtype=jnp.float32) * (2.0 / head_dim)
    frequency = jnp.power(jnp.float32(ROPE_BASE), -exponent)
    angles = positions.astype(jnp.float32)[:, None] * frequency[None, :]
    cosine = jnp.cos(angles)[:, None, :]
    sine_part = jnp.sin(angles)[:, None, :]
    lower_half = values[..., :half_dim]
    upper_half = values[..., half_dim:]
    return jnp.concatenate(
        [
            lower_half * cosine - upper_half * sine_part,
            upper_half * cosine + lower_half * sine_part,
        ],
        axis=-1,
    )


def attend_keys(running, query_rows, row_pos, row_seg, key_rows, value_rows, key_pos, key_seg):
    heads_kv = query_rows.shape[0]
    head_dim = query_rows.shape[2]
    key_count = key_rows.shape[0]
    block_rows = math.gcd(key_count, 512)
    block_count = key_count // block_rows
    score_scale = 1.0 / math.sqrt(head_dim)
    keys_three = key_rows.reshape(key_count, heads_kv, head_dim)
    values_three = value_rows.reshape(key_count, heads_kv, head_dim)

    def one_block(index_block, state):
        highest, totals, weighted = state
        first_row = index_block * block_rows
        key_block = lax.dynamic_slice_in_dim(keys_three, first_row, block_rows, 0)
        value_block = lax.dynamic_slice_in_dim(values_three, first_row, block_rows, 0)
        pos_block = lax.dynamic_slice_in_dim(key_pos, first_row, block_rows, 0)
        seg_block = lax.dynamic_slice_in_dim(key_seg, first_row, block_rows, 0)
        scores = (
            jnp.einsum("hrd,nhd->hrn", query_rows, key_block, preferred_element_type=jnp.float32)
            * score_scale
        )
        allowed = (pos_block[None, :] <= row_pos[:, None]) & (
            seg_block[None, :] == row_seg[:, None]
        )
        new_high = jnp.maximum(
            highest, jnp.max(jnp.where(allowed[None], scores, NEG_FILL), axis=-1)
        )
        weights = jnp.where(allowed[None], jnp.exp(scores - new_high[..., None]), 0.0)
        rescale = jnp.exp(highest - new_high)
        totals = totals * rescale + jnp.sum(weights, axis=-1)
        added = jnp.einsum(
            "hrn,nhd->hrd",
            weights.astype(jnp.bfloat16),
            value_block,
            preferred_element_type=jnp.float32,
        )
        weighted = weighted * rescale[..., None] + added
        return (new_high, totals, weighted)

    return lax.fori_loop(0, block_count, one_block, running)


def body(hidden_states, w_query, w_key, w_value, w_out, span_order, lengths):
    tok_rows = hidden_states.shape[0]
    half_rows = tok_rows // 2
    ctx_count = lax.axis_size("ctx")
    own_index = lax.axis_index("ctx")
    offsets = jnp.arange(half_rows, dtype=jnp.int32)
    pos_table = (span_order[:, None] * half_rows + offsets[None, :]).reshape(ctx_count, tok_rows)
    boundaries = jnp.cumsum(lengths)[:-1]

    def segment_of(positions):
        return jnp.sum((positions[:, None] >= boundaries[None, :]).astype(jnp.int32), axis=1)

    own_pos = lax.dynamic_index_in_dim(pos_table, own_index, 0, keepdims=False)
    own_seg = segment_of(own_pos)
    piece = lax.all_gather(hidden_states, "tp", axis=1, tiled=True)
    queries = jnp.dot(piece, w_query, preferred_element_type=jnp.float32)
    keys_raw = jnp.dot(piece, w_key, preferred_element_type=jnp.float32)
    values_raw = jnp.dot(piece, w_value, preferred_element_type=jnp.float32)
    head_dim = HEAD_DIM
    group_size = HEADS // KV_HEADS
    heads_kv = keys_raw.shape[1] // head_dim
    q_rot = rotate_half(queries.reshape(tok_rows, heads_kv * group_size, head_dim), own_pos).astype(
        jnp.bfloat16
    )
    q_rot = (
        q_rot.reshape(tok_rows, heads_kv, group_size, head_dim)
        .transpose(1, 2, 0, 3)
        .reshape(heads_kv, group_size * tok_rows, head_dim)
    )
    k_rot = (
        rotate_half(keys_raw.reshape(tok_rows, heads_kv, head_dim), own_pos)
        .astype(jnp.bfloat16)
        .reshape(tok_rows, heads_kv * head_dim)
    )
    v_rows = values_raw.astype(jnp.bfloat16)
    row_pos = jnp.tile(own_pos, group_size)
    row_seg = jnp.tile(own_seg, group_size)
    query_count = group_size * tok_rows
    running = (
        jnp.full((heads_kv, query_count), NEG_FILL, jnp.float32),
        jnp.zeros((heads_kv, query_count), jnp.float32),
        jnp.zeros((heads_kv, query_count, head_dim), jnp.float32),
    )
    flat_pos = pos_table.reshape(-1)
    running = attend_keys(
        running,
        q_rot,
        row_pos,
        row_seg,
        lax.all_gather(k_rot, "ctx", axis=0, tiled=True),
        lax.all_gather(v_rows, "ctx", axis=0, tiled=True),
        flat_pos,
        segment_of(flat_pos),
    )
    highest, totals, weighted = running
    context = (weighted / totals[..., None]).astype(jnp.bfloat16)
    context = (
        context.reshape(heads_kv, group_size, tok_rows, head_dim)
        .transpose(2, 0, 1, 3)
        .reshape(tok_rows, heads_kv * group_size * head_dim)
    )
    partial_value = jnp.dot(context, w_out, preferred_element_type=jnp.float32)
    return lax.psum_scatter(
        partial_value.astype(jnp.bfloat16), "tp", scatter_dimension=1, tiled=True
    )


def solution(mesh):
    in_specs = (
        P("ctx", "tp"),
        P(None, "tp"),
        P(None, "tp"),
        P(None, "tp"),
        P("tp", None),
        P(),
        P(),
    )
    out_specs = P("ctx", "tp")
    return jax.shard_map(body, mesh=mesh, in_specs=in_specs, out_specs=out_specs, check_vma=False)
```

profile of v0, /device:TPU:96, one launch (start us, length us, event | category | flops | bytes accessed | tf_op | source)
XLA Modules:
  0.0 358.2 jit_solution(8336135585316746964)
XLA Ops:
  7.3 57.1 %all-gather.4.cloned.1.call-done = bf16[256,4096]{1,0:T(8,128)(2,1)} async-done(((bf16[256,512]{1,0:T(8,128)(2,1)}), bf16[256,4096]{1,0:T(8,128)(2,1)}) %all-gather.4.cloned.1.call-update) | async-done | bytes 2097168 | tf_op jit(solution)/shard_map/all_gather | solution.py:92
  64.5 3.1 convolution_convert_fusion.1
  67.9 2.0 convolution_bitcast_fusion.1
  72.1 4.2 %fusion.42 = f32[256,512]{1,0:T(8,128)} fusion(bf16[256,4096]{1,0:T(8,128)(2,1)S(1)} %copy-done.1, bf16[4096,512]{1,0:T(8,128)(2,1)} %param.10), kind=kOutput, calls=%fused_computation.70 | convolution fusion | flops 1073741824 | bytes 6815744 | tf_op jit(solution)/shard_map/dot_general | solution.py:93
  78.5 69.0 %all-gather.8.cloned.1.call-done = bf16[8192,128]{1,0:T(8,128)(2,1)} async-done(((bf16[256,128]{1,0:T(8,128)(2,1)}), bf16[8192,128]{1,0:T(8,128)(2,1)}) %all-gather.8.cloned.1.call-update) | async-done | bytes 2097168 | tf_op jit(solution)/shard_map/all_gather | solution.py:128
  147.5 75.9 %all-gather.6.cloned.1.call-done = bf16[8192,128]{0,1:T(8,128)(2,1)} async-done(((bf16[256,128]{0,1:T(8,128)(2,1)}), bf16[8192,128]{0,1:T(8,128)(2,1)}) %all-gather.6.cloned.1.call-update) | async-done | bytes 2097168 | tf_op jit(solution)/shard_map/all_gather | solution.py:127
  223.4 71.1 %while.18 = (s32[]{:T(128)}, f32[1,1024]{1,0:T(1,128)S(1)}, f32[1,1024]{1,0:T(1,128)S(1)}, f32[1,1024,128]{2,1,0:T(8,128)S(1)}, s32[8192]{0:T(1024)S(1)}, /*inde...) while((s32[]{:T(128)}, f32[1,1024]{1,0:T(1,128)S(1)}, ...), condition=%wide.region_6.7_spmd.clone, body=%wide.region_3.6_spmd.clone.sunk | while | flops 279319552 | bytes 8001759 | solution.py:75
  225.8 1.9 fusion.64
  228.0 1.6 fusion.60
  230.3 1.9 fusion.64
  232.4 1.6 fusion.60
  234.7 1.9 fusion.64
  239.2 1.9 fusion.64
  241.3 1.6 fusion.60
  243.6 1.9 fusion.64
  248.1 1.9 fusion.64
  250.2 1.6 fusion.60
  252.5 1.9 fusion.64
  257.0 1.9 fusion.64
  259.1 1.6 fusion.60
  261.4 1.9 fusion.64
  265.8 1.9 fusion.64
  268.0 1.6 fusion.60
  270.3 1.9 fusion.64
  274.7 1.9 fusion.64
  276.9 1.6 fusion.60
  279.2 1.9 fusion.64
  283.6 1.9 fusion.64
  288.1 1.9 fusion.64
  292.5 1.9 fusion.64
  294.9 4.8 %convolution_convert_fusion = bf16[256,4096]{1,0:T(8,128)(2,1)} fusion(bf16[256,512]{0,1:T(8,128)(2,1)S(1)} %bitcast.113, bf16[512,4096]{1,0:T(8,128)(2,1)} %param.13), kind=kOutput, calls=%fused_computation.37 | convolution fusion | flops 1074790400 | bytes 6553600 | tf_op jit(solution)/shard_map/dot_general | solution.py:139
  299.7 52.0 %reduce-scatter.2.cloned.1.call-done = bf16[256,512]{1,0:T(8,128)(2,1)} async-done(((bf16[256,4096]{1,0:T(8,128)(2,1)}), bf16[256,512]{1,0:T(8,128)(2,1)}) %reduce-scatter.2.cloned.1.call-update) | async-done | bytes 262160 | tf_op jit(solution)/shard_map/reduce_scatter | solution.py:140
  (196 shorter events, 33.6 us)
Async XLA Ops:
  6.5 57.9 %copy-start = (bf16[4096,128]{1,0:T(8,128)(2,1)S(1)}, bf16[4096,128]{1,0:T(8,128)(2,1)}, u32[]{:S(2)}) copy-start(bf16[4096,128]{1,0:T(8,128)(2,1)} %param.12) | copy-start | bytes 3145732
  6.5 61.1 %copy-start.3 = (s32[64]{0:T(128)S(1)}, s32[64]{0:T(128)}, u32[]{:S(2)}) copy-start(s32[64]{0:T(128)} %param.14) | copy-start | bytes 772
  6.5 57.9 %all-gather.4.cloned.1.call-start = ((), (), s32[]{:S(2)}) async-start(), calls=%async_computation.1 | async-start | bytes 2359296 | tf_op jit(solution)/shard_map/all_gather | solution.py:92
  7.3 140.2 %all-gather.8.cloned.1.call-start = ((), (), s32[]{:S(2)}) async-start(), calls=%async_computation.3 | async-start | bytes 2162688 | tf_op jit(solution)/shard_map/all_gather | solution.py:128
  64.5 3.4 copy-start.1
  67.5 3.5 copy-start.4
  67.5 155.8 %all-gather.6.cloned.1.call-start = ((), (), s32[]{:S(2)}) async-start(), calls=%async_computation.2 | async-start | bytes 2162688 | tf_op jit(solution)/shard_map/all_gather | solution.py:127
  71.0 280.7 %reduce-scatter.2.cloned.1.call-start = ((), (), s32[]{:S(2)}) async-start(), calls=%async_computation.4 | async-start | bytes 2359296 | tf_op jit(solution)/shard_map/reduce_scatter | solution.py:140
  76.3 147.0 %copy-start.2 = (f32[1,1024,128]{2,1,0:T(8,128)S(1)}, f32[1,1024,128]{2,1,0:T(8,128)}, u32[]{:S(2)}) copy-start(f32[1,1024,128]{2,1,0:T(8,128)} %custom-call.2) | copy-start | bytes 1572868
Sparse Core Ops, SparseCore 0:
  9.2 55.2 all-gather.3
  67.7 79.7 all-gather.7
  150.1 73.2 all-gather.5
  299.8 51.8 reduce-scatter.1
where the time goes:
time: 360 us; the launch traced here: 358 us
  waiting for transfers between devices  255 us (71%)
  matrix products  70.9 us (20%)
  other arithmetic  13.8 us (4%)
  between operations  13.3 us (4%)
  local copies, waits for them, and re-layouts  4.32 us (1%)
    all_gather x1, waiting for transfers between devices, body(): lax.all_gather(k_rot, 'ctx', axis=0, tiled=True)  75.9 us
    all_gather x1, waiting for transfers between devices, body(): lax.all_gather(v_rows, 'ctx', axis=0, tiled=True)  69 us
    all_gather x1, waiting for transfers between devices, body(): piece = lax.all_gather(hidden_states, 'tp', axis=1, tiled=True)  57.1 us
    reduce_scatter x1, waiting for transfers between devices, body(): lax.psum_scatter(partial_value.astype(jnp.bfloat16), 'tp', scatter_dimens...  52 us
    dot_general x16, matrix products, one_block(): jnp.einsum('hrn,nhd->hrd', weights.astype(jnp.bfloat16), value_block, pre...  30.9 us
    dot_general x16, matrix products, one_block(): jnp.einsum('hrd,nhd->hrn', query_rows, key_block, preferred_element_type=...  25.8 us
    reduce_sum x16, other arithmetic, one_block(): totals = totals * rescale + jnp.sum(weights, axis=-1)  10.2 us
  transfers between devices with their start and end apart: 4, of which 4 were waited for; matrix products, arithmetic and copies ran while one was open for 3% of the time, Pallas kernels for 0%

commit v1 on v0

v1 whole, which is shorter than its diff:
```python
import functools
import math

import jax
import jax.numpy as jnp
from jax import lax
from jax.experimental import pallas as pl
from jax.experimental.pallas import tpu as pltpu
from jax.sharding import PartitionSpec as P

HEADS = 32
KV_HEADS = 8
HEAD_DIM = 128
GROUP = HEADS // KV_HEADS
SPAN = 128
SEQ = 8192
D = 4096
N_CTX = 32
N_TP = 8
FEATS = D // N_TP
ROWS = SEQ // N_CTX
BLOCKS = SEQ // SPAN
STEP = 4

ROPE_BASE = 500000.0
MASKED = -1e30
LOWEST = -1e29
SCALE = math.log2(math.e) / math.sqrt(HEAD_DIM)


def vmem():
    return pl.BlockSpec(memory_space=pltpu.VMEM)


def smem():
    return pl.BlockSpec(memory_space=pltpu.SMEM)


def rotate(values, cosine, sine):
    return values * cosine + pltpu.roll(values, HEAD_DIM // 2, 1) * sine


def project(first, pieces, w_ref):
    total = None
    for k, piece in enumerate(pieces):
        row = pl.multiple_of(lax.rem(first + k, N_TP) * FEATS, FEATS)
        part = jnp.dot(piece[...], w_ref[pl.ds(row, FEATS), :], preferred_element_type=jnp.float32)
        total = part if total is None else total + part
    return total


def kv_kernel(me_ref, *refs):
    pieces, (wk_ref, wv_ref, cos_ref, sin_ref, out_ref) = refs[:N_TP], refs[N_TP:]
    keys = project(me_ref[0], pieces, wk_ref)
    out_ref[:, :HEAD_DIM] = rotate(keys, cos_ref[...], sin_ref[...]).astype(jnp.bfloat16)
    out_ref[:, HEAD_DIM:] = project(me_ref[0], pieces, wv_ref).astype(jnp.bfloat16)


def q_kernel(me_ref, *refs):
    pieces, (wq_ref, cos_ref, sin_ref, out_ref) = refs[:N_TP], refs[N_TP:]
    queries = project(me_ref[0], pieces, wq_ref)
    for h in range(GROUP):
        cols = slice(h * HEAD_DIM, (h + 1) * HEAD_DIM)
        out_ref[:, cols] = rotate(queries[:, cols], cos_ref[...], sin_ref[...]).astype(jnp.bfloat16)


def attend_kernel(slot_ref, span_ref, bounds_ref, q_ref, kv_ref, out_ref, q_sc, m_sc, acc_sc):
    rows = GROUP * SPAN
    keys = STEP * SPAN
    ones = jnp.ones((keys, HEAD_DIM), jnp.bfloat16)

    def start_of(position):
        start = jnp.int32(0)
        for i in range(3):
            start = jnp.where(bounds_ref[i] <= position, bounds_ref[i], start)
        return start

    for b in range(ROWS // SPAN):
        for h in range(GROUP):
            q_sc[h * SPAN:(h + 1) * SPAN, :] = q_ref[b * SPAN:(b + 1) * SPAN, h * HEAD_DIM:(h + 1) * HEAD_DIM]
        m_sc[...] = jnp.full(m_sc.shape, LOWEST, jnp.float32)
        acc_sc[...] = jnp.zeros(acc_sc.shape, jnp.float32)
        own = span_ref[b]
        low = start_of(own * SPAN) // SPAN
        last_start = start_of(own * SPAN + SPAN - 1)
        count = (own - low) // STEP + 1
        plain_from = jnp.minimum((last_start - low * SPAN + keys - 1) // keys, count - 1)
        plain_from = jnp.maximum(plain_from, 0)
        row_pos = own * SPAN + lax.broadcasted_iota(jnp.int32, (rows, 1), 0) % SPAN
        row_start = jnp.zeros((rows, 1), jnp.int32)
        for i in range(3):
            row_start = jnp.where(bounds_ref[i] <= row_pos, bounds_ref[i], row_start)

        def step(i, masked):
            first = low + i * STEP
            parts = [
                kv_ref[pl.ds(pl.multiple_of(slot_ref[jnp.minimum(first + g, own)] * SPAN, SPAN), SPAN), :]
                for g in range(STEP)
            ]
            k = jnp.concatenate([p[:, :HEAD_DIM] for p in parts], axis=0)
            v = jnp.concatenate([p[:, HEAD_DIM:] for p in parts], axis=0)
            v = jnp.concatenate([v, ones], axis=1)
            scores = lax.dot_general(q_sc[...], k, (((1,), (1,)), ((), ())), preferred_element_type=jnp.float32) * SCALE
            if masked:
                key_pos = first * SPAN + lax.broadcasted_iota(jnp.int32, (rows, keys), 1)
                scores = jnp.where((key_pos <= row_pos) & (key_pos >= row_start), scores, MASKED)
            old = m_sc[...]
            new = jnp.maximum(old, jnp.max(scores, axis=1, keepdims=True))
            m_sc[...] = new
            weights = jnp.exp2(scores - jnp.concatenate([new] * STEP, axis=1)).astype(jnp.bfloat16)
            alpha = jnp.exp2(old - new)
            acc_sc[...] = acc_sc[...] * jnp.concatenate([alpha, alpha], axis=1) + jnp.dot(
                weights, v, preferred_element_type=jnp.float32
            )

        def loop(masked):
            def body(i, carry):
                step(i, masked)
                return carry

            return body

        lax.fori_loop(0, plain_from, loop(True), 0)
        lax.fori_loop(plain_from, count - 1, loop(False), 0)
        lax.fori_loop(count - 1, count, loop(True), 0)
        for h in range(GROUP):
            part = slice(h * SPAN, (h + 1) * SPAN)
            out_ref[b * SPAN:(b + 1) * SPAN, h * HEAD_DIM:(h + 1) * HEAD_DIM] = (
                acc_sc[part, :HEAD_DIM] / acc_sc[part, HEAD_DIM:]
            ).astype(jnp.bfloat16)


def out_kernel(ctx_ref, w_ref, out_ref):
    for j in range(N_TP):
        out_ref[j] = jnp.dot(
            ctx_ref[...], w_ref[:, j * FEATS:(j + 1) * FEATS], preferred_element_type=jnp.float32
        ).astype(jnp.bfloat16)


def call(kernel, shape, in_specs, scratch=(), vmem_mb=40, flops=0, nbytes=0):
    return pl.pallas_call(
        kernel,
        out_shape=shape,
        in_specs=in_specs,
        out_specs=vmem(),
        scratch_shapes=list(scratch),
        compiler_params=pltpu.CompilerParams(vmem_limit_bytes=vmem_mb << 20),
        cost_estimate=pl.CostEstimate(flops=flops, bytes_accessed=nbytes, transcendentals=0),
    )


def body(hidden_states, w_query, w_key, w_value, w_out, span_order, lengths):
    own_ctx = lax.axis_index("ctx")
    own_tp = lax.axis_index("tp")
    me = own_tp.reshape(1)

    with jax.named_scope("gather_hidden"):
        pieces = [hidden_states] + [
            lax.ppermute(hidden_states, "tp", [(i, (i - k) % N_TP) for i in range(N_TP)]) for k in range(1, N_TP)
        ]

    own_spans = lax.dynamic_slice_in_dim(span_order, own_ctx * 2, 2, 0)
    positions = (own_spans[:, None] * SPAN + jnp.arange(SPAN, dtype=jnp.int32)[None, :]).reshape(ROWS)
    half = HEAD_DIM // 2
    frequency = jnp.power(jnp.float32(ROPE_BASE), -(jnp.arange(half, dtype=jnp.float32) * (2.0 / HEAD_DIM)))
    angles = positions.astype(jnp.float32)[:, None] * frequency[None, :]
    cosine, sine = jnp.cos(angles), jnp.sin(angles)
    cosine = jnp.concatenate([cosine, cosine], axis=1)
    sine = jnp.concatenate([-sine, sine], axis=1)

    kv = call(
        kv_kernel,
        jax.ShapeDtypeStruct((ROWS, 2 * HEAD_DIM), jnp.bfloat16),
        [smem()] + [vmem()] * (N_TP + 4),
        flops=2 * ROWS * D * 2 * HEAD_DIM,
        nbytes=4 << 20,
    )(me, *pieces, w_key, w_value, cosine, sine)

    with jax.named_scope("gather_kv"):
        other = lax.ppermute(kv, "ctx", [(i, i ^ 2) for i in range(N_CTX)])
        column = jnp.concatenate([kv, other], axis=0)
        up = down = column
        rings = [column]
        for _ in range(3):
            up = lax.ppermute(up, "ctx", [(i, (i + 4) % N_CTX) for i in range(N_CTX)])
            down = lax.ppermute(down, "ctx", [(i, (i - 4) % N_CTX) for i in range(N_CTX)])
            rings += [up, down]
        up = lax.ppermute(up[:ROWS], "ctx", [(i, (i + 4) % N_CTX) for i in range(N_CTX)])
        down = lax.ppermute(down[ROWS:], "ctx", [(i, (i - 4) % N_CTX) for i in range(N_CTX)])
        rings += [up, down]
        flip = [(i, i ^ 1) for i in range(N_CTX)]
        mine = jnp.concatenate(rings, axis=0)
        theirs = [lax.ppermute(r, "ctx", flip) for r in rings]
        keys_values = jnp.concatenate([mine] + theirs, axis=0)

    base_z, low_bits = own_ctx // 4, own_ctx % 4
    offsets = jnp.array([0, 0, -1, -1, 1, 1, -2, -2, 2, 2, -3, -3, 3, 3, 4, 4], jnp.int32)
    flips = jnp.array([0, 2] * 8, jnp.int32)
    source = ((base_z + offsets) % 8) * 4 + (low_bits ^ flips)
    source = jnp.concatenate([source, source ^ 1])
    source_block = (source[:, None] * 2 + jnp.arange(2, dtype=jnp.int32)[None, :]).reshape(BLOCKS)
    slot_of_block = jnp.sum(
        jnp.where(source_block[None, :] == jnp.arange(BLOCKS, dtype=jnp.int32)[:, None], jnp.arange(BLOCKS, dtype=jnp.int32)[None, :], 0),
        axis=1,
    )
    slots = jnp.sum(
        jnp.where(span_order[None, :] == jnp.arange(BLOCKS, dtype=jnp.int32)[:, None], slot_of_block[None, :], 0), axis=1
    ).astype(jnp.int32)
    bounds = jnp.stack([lengths[0], lengths[0] + lengths[1], lengths[0] + lengths[1] + lengths[2]]).astype(jnp.int32)

    queries = call(
        q_kernel,
        jax.ShapeDtypeStruct((ROWS, GROUP * HEAD_DIM), jnp.bfloat16),
        [smem()] + [vmem()] * (N_TP + 3),
        flops=2 * ROWS * D * GROUP * HEAD_DIM,
        nbytes=6 << 20,
    )(me, *pieces, w_query, cosine, sine)

    context = call(
        attend_kernel,
        jax.ShapeDtypeStruct((ROWS, GROUP * HEAD_DIM), jnp.bfloat16),
        [smem()] * 3 + [vmem()] * 2,
        scratch=[
            pltpu.VMEM((GROUP * SPAN, HEAD_DIM), jnp.bfloat16),
            pltpu.VMEM((GROUP * SPAN, HEAD_DIM), jnp.float32),
            pltpu.VMEM((GROUP * SPAN, 2 * HEAD_DIM), jnp.float32),
        ],
        flops=4 * ROWS * GROUP * 4096 * HEAD_DIM,
        nbytes=5 << 20,
    )(slots, own_spans, bounds, queries, keys_values)

    partial = call(
        out_kernel,
        jax.ShapeDtypeStruct((N_TP, ROWS, FEATS), jnp.bfloat16),
        [vmem()] * 2,
        flops=2 * ROWS * GROUP * HEAD_DIM * D,
        nbytes=6 << 20,
    )(context, w_out)
    with jax.named_scope("scatter_out"):
        shares = lax.all_to_all(partial, "tp", 0, 0, tiled=True)
        return jnp.sum(shares.astype(jnp.float32), axis=0).astype(jnp.bfloat16)


def solution(mesh):
    in_specs = (
        P("ctx", "tp"),
        P(None, "tp"),
        P(None, "tp"),
        P(None, "tp"),
        P("tp", None),
        P(),
        P(),
    )
    return jax.shard_map(body, mesh=mesh, in_specs=in_specs, out_specs=P("ctx", "tp"), check_vma=False)
```

time: 360 us -> 127 us (0.35)
  waiting for transfers between devices: 255 us -> 43 us
  matrix products: 70.9 us -> 0 us
  starting transfers between devices: 0.13 us -> 28.2 us
  blocking collectives: 0 us -> 25.7 us
  Pallas kernels: 0 us -> 16.6 us
  between operations: 13.3 us -> 2.25 us
  other arithmetic: 13.8 us -> 4.29 us
    all_gather x3 -> x0, waiting for transfers between devices: 202 us -> none  [the longest x1 75.9 us: body(): lax.all_gather(k_rot, 'ctx', axis=0, tiled=True)]
    dot_general x36 -> x0, matrix products: 70.9 us -> none  [the longest x16 30.9 us: one_block(): jnp.einsum('hrn,nhd->hrd', weights.astype(jnp.bfloat16), value_block, pre...]
    reduce_scatter x1 -> x0, waiting for transfers between devices: 52 us -> none  [body(): lax.psum_scatter(partial_value.astype(jnp.bfloat16), 'tp', scatter_dimens...]
    ppermute x0 -> x25, waiting for transfers between devices: none -> 43 us  [the longest x7 24.1 us: body(): lax.ppermute(hidden_states, 'tp', [(i, (i - k) % N_TP) for i in range(N_T...]
    ppermute x0 -> x25, starting transfers between devices: none -> 28.2 us  [the longest x3 10.2 us: body(): up = lax.ppermute(up, 'ctx', [(i, (i + 4) % N_CTX) for i in range(N_CTX)])]
    all_to_all x0 -> x1, blocking collectives: none -> 25.7 us  [body(): shares = lax.all_to_all(partial, 'tp', 0, 0, tiled=True)]
    pallas_call x0 -> x4, Pallas kernels: none -> 16.6 us  [the longest x1 12.7 us: body(): call(attend_kernel, jax.ShapeDtypeStruct((ROWS, GROUP * HEAD_DIM), jnp.bf...]
    reduce_sum x18 -> x3, other arithmetic: 10.5 us -> 1.26 us  [the longest x1 1.05 us: body(): return jnp.sum(shares.astype(jnp.float32), axis=0).astype(jnp.bfloat16)]
  transfers between devices with their start and end apart: 4 -> 25, of which waited for: 4 -> 15; matrix products, arithmetic and copies ran while one was open for 3% -> 3% of each run, Pallas kernels for 0% -> 1%
where the time goes in v1:
time: 127 us
  waiting for transfers between devices  43 us (34%)
  starting transfers between devices  28.2 us (22%)
  blocking collectives  25.7 us (20%)
  Pallas kernels  16.6 us (13%)
  local copies, waits for them, and re-layouts  6.69 us (5%)
  other arithmetic  4.29 us (3%)
  between operations  2.25 us (2%)
    all_to_all x1, blocking collectives, body(): shares = lax.all_to_all(partial, 'tp', 0, 0, tiled=True)  25.7 us
    ppermute x7, waiting for transfers between devices, body(): lax.ppermute(hidden_states, 'tp', [(i, (i - k) % N_TP) for i in range(N_T...  24.1 us
    pallas_call x1, Pallas kernels, body(): call(attend_kernel, jax.ShapeDtypeStruct((ROWS, GROUP * HEAD_DIM), jnp.bf...  12.7 us
    ppermute x3, waiting for transfers between devices, body(): up = lax.ppermute(up, 'ctx', [(i, (i + 4) % N_CTX) for i in range(N_CTX)])  10.6 us
    ppermute x3, starting transfers between devices, body(): up = lax.ppermute(up, 'ctx', [(i, (i + 4) % N_CTX) for i in range(N_CTX)])  10.2 us
    ppermute x7, starting transfers between devices, body(): lax.ppermute(hidden_states, 'tp', [(i, (i - k) % N_TP) for i in range(N_T...  8.85 us
    unnamed x34, local copies, waits for them, and re-layouts  5.9 us
    ppermute x1, starting transfers between devices, body(): lax.ppermute(up[:ROWS], 'ctx', [(i, (i + 4) % N_CTX) for i in range(N_CTX)])  3.77 us
  transfers between devices with their start and end apart: 25, of which 15 were waited for; matrix products, arithmetic and copies ran while one was open for 3% of the time, Pallas kernels for 1%

profile of v1, /device:TPU:96, one launch (start us, length us, event | category | flops | bytes accessed | tf_op | source)
XLA Modules:
  0.0 126.8 jit_solution(10591464446049838762)
XLA Ops:
  0.0 3.8 %collective-permute-start = (bf16[256,512]{1,0:T(8,128)(2,1)}, bf16[256,512]{1,0:T(8,128)(2,1)S(1)}, u32[]{:S(2)}, u32[]{:S(2)}) collective-permute-start(bf16[256,512]{1,0:T(8,128)(2,1)} %refs_0_.3), channel_id=1, source_target_pairs={{0,7},{1,0},{2,1},{3,2},{4,3},{5,4},{6,5},{7,6},{8,15},{9,8},{10,9... | collective-permute-start | bytes 786440 | tf_op jit(solution)/shard_map/gather_hidden/ppermute | solution.py:159
  3.9 0.8 collective-permute-start.1
  5.1 2.7 %collective-permute-start.3 = (bf16[256,512]{1,0:T(8,128)(2,1)}, bf16[256,512]{1,0:T(8,128)(2,1)S(1)}, u32[]{:S(2)}, u32[]{:S(2)}) collective-permute-start(bf16[256,512]{1,0:T(8,128)(2,1)} %refs_0_.3), channel_id=1, source_target_pairs={{0,4},{1,5},{2,6},{3,7},{4,0},{5,1},{6,2},{7,3},{8,12},{9,13},{10,... | collective-permute-start | bytes 786440 | tf_op jit(solution)/shard_map/gather_hidden/ppermute | solution.py:159
  7.9 0.7 broadcast_multiply_fusion
  9.4 0.7 broadcast_xor_fusion
  10.1 0.8 collective-permute-done.refs_1_
  10.9 1.0 collective-permute-start.5
  11.9 14.7 %collective-permute-done.1.refs_2_ = bf16[256,512]{1,0:T(8,128)(2,1)S(1)} collective-permute-done((bf16[256,512]{1,0:T(8,128)(2,1)}, bf16[256,512]{1,0:T(8,128)(2,1)S(1)}, u32[]{:S(2)}, u32[]{:S(2)}) %collective-permute-start.1) | collective-permute-done | bytes 262176 | tf_op jit(solution)/shard_map/gather_hidden/ppermute | solution.py:159
  26.8 2.9 %collective-permute-done.4.refs_5_ = bf16[256,512]{1,0:T(8,128)(2,1)S(1)} collective-permute-done((bf16[256,512]{1,0:T(8,128)(2,1)}, bf16[256,512]{1,0:T(8,128)(2,1)S(1)}, u32[]{:S(2)}, u32[]{:S(2)}) %collective-permute-start.4) | collective-permute-done | bytes 262176 | tf_op jit(solution)/shard_map/gather_hidden/ppermute | solution.py:159
  29.7 3.9 %collective-permute-done.5.refs_6_ = bf16[256,512]{1,0:T(8,128)(2,1)S(1)} collective-permute-done((bf16[256,512]{1,0:T(8,128)(2,1)}, bf16[256,512]{1,0:T(8,128)(2,1)S(1)}, u32[]{:S(2)}, u32[]{:S(2)}) %collective-permute-start.5) | collective-permute-done | bytes 262176 | tf_op jit(solution)/shard_map/gather_hidden/ppermute | solution.py:159
  33.6 1.7 %collective-permute-done.6.refs_7_ = bf16[256,512]{1,0:T(8,128)(2,1)S(1)} collective-permute-done((bf16[256,512]{1,0:T(8,128)(2,1)}, bf16[256,512]{1,0:T(8,128)(2,1)S(1)}, u32[]{:S(2)}, u32[]{:S(2)}) %collective-permute-start.6) | collective-permute-done | bytes 262176 | tf_op jit(solution)/shard_map/gather_hidden/ppermute | solution.py:159
  35.3 1.2 copy-done.2
  36.5 1.2 copy-done.3
  37.8 0.9 copy-done.4
  38.7 1.3 %shard_map.92 = bf16[256,256]{1,0:T(8,128)(2,1)S(1)} custom-call(s32[1]{0:T(128)} %bitcast.me_ref, bf16[256,512]{1,0:T(8,128)(2,1)S(1)} %copy-done.4, bf16[256,512]{1,0:T(8,128)(2,1)S(1)} %collective-permute-done.refs_1_, bf16[256,512]{1,0:T(8,128)(2,1)S(1)} %collective-permute-done.1.refs_2_, bf16[256,512]{1,0:T(8,128)(2,1)S(1)} %collective-permute-done.2.refs_3_, ...), custom_call_target="tpu_custom_call" | custom-call | flops 536870912 | bytes 4194304 | tf_op jit(solution)/shard_map/pallas_call | solution.py:171
  40.0 3.0 %collective-permute-start.7 = (bf16[256,256]{1,0:T(8,128)(2,1)S(1)}, bf16[256,256]{1,0:T(8,128)(2,1)S(1)}, u32[]{:S(2)}, u32[]{:S(2)}) collective-permute-start(bf16[256,256]{1,0:T(8,128)(2,1)S(1)} %shard_map.92), channel_id=1, source_target_pairs={{0,16},{8,24},{16,0},{24,8},{32,48},{40,56},{48,32},{56,40},{64,80... | collective-permute-start | bytes 393224 | tf_op jit(solution)/shard_map/gather_kv/ppermute | solution.py:180
  45.8 0.7 collective-permute-done.7
  46.6 3.2 %collective-permute-start.8 = (bf16[512,256]{1,0:T(8,128)(2,1)S(1)}, bf16[512,256]{1,0:T(8,128)(2,1)S(1)}, u32[]{:S(2)}, u32[]{:S(2)}) collective-permute-start(bf16[512,256]{1,0:T(8,128)(2,1)S(1)} %pad_maximum_fusion), channel_id=1, source_target_pairs={{0,32},{8,40},{16,48},{24,56},{32,64},{40,72},{48,80},{56,88},{64,... | collective-permute-start | bytes 786440 | tf_op jit(solution)/shard_map/gather_kv/ppermute | solution.py:185
  49.8 0.7 pad_add_fusion.bounds_ref
  50.6 4.5 %collective-permute-done.8 = bf16[512,256]{1,0:T(8,128)(2,1)S(1)} collective-permute-done((bf16[512,256]{1,0:T(8,128)(2,1)S(1)}, bf16[512,256]{1,0:T(8,128)(2,1)S(1)}, u32[]{:S(2)}, u32[]{:S(2)}) %collective-permute-start.8) | collective-permute-done | bytes 262176 | tf_op jit(solution)/shard_map/gather_kv/ppermute | solution.py:185
  55.1 3.7 %collective-permute-start.10 = (bf16[512,256]{1,0:T(8,128)(2,1)S(1)}, bf16[512,256]{1,0:T(8,128)(2,1)S(1)}, u32[]{:S(2)}, u32[]{:S(2)}) collective-permute-start(bf16[512,256]{1,0:T(8,128)(2,1)S(1)} %collective-permute-done.8), channel_id=1, source_target_pairs={{0,32},{8,40},{16,48},{24,56},{32,64},{40,72},{48,80},{56,88},{64,... | collective-permute-start | bytes 786440 | tf_op jit(solution)/shard_map/gather_kv/ppermute | solution.py:185
  59.2 2.2 %copy-done = bf16[4096,512]{1,0:T(8,128)(2,1)S(1)} copy-done((bf16[4096,512]{1,0:T(8,128)(2,1)S(1)}, bf16[4096,512]{1,0:T(8,128)(2,1)}, u32[]{:S(2)}) %copy-start) | copy-done | bytes 4194328
  61.3 1.4 %shard_map.91.q_ref = bf16[256,512]{1,0:T(8,128)(2,1)S(1)} custom-call(s32[1]{0:T(128)} %bitcast.me_ref, bf16[256,512]{1,0:T(8,128)(2,1)S(1)} %copy-done.5, bf16[256,512]{1,0:T(8,128)(2,1)S(1)} %collective-permute-done.refs_1_, bf16[256,512]{1,0:T(8,128)(2,1)S(1)} %collective-permute-done.1.refs_2_, bf16[256,512]{1,0:T(8,128)(2,1)S(1)} %collective-permute-done.2.refs_3_, ...), custom_call_target="tpu_custom_call" | custom-call | flops 1073741824 | bytes 6291456 | tf_op jit(solution)/shard_map/pallas_call | solution.py:211
  63.7 3.3 %collective-permute-start.12 = (bf16[512,256]{1,0:T(8,128)(2,1)S(1)}, bf16[512,256]{1,0:T(8,128)(2,1)S(1)}, u32[]{:S(2)}, u32[]{:S(2)}) collective-permute-start(bf16[512,256]{1,0:T(8,128)(2,1)S(1)} %collective-permute-done.10), channel_id=1, source_target_pairs={{0,32},{8,40},{16,48},{24,56},{32,64},{40,72},{48,80},{56,88},{64,... | collective-permute-start | bytes 786440 | tf_op jit(solution)/shard_map/gather_kv/ppermute | solution.py:185
  67.1 6.1 %collective-permute-done.12 = bf16[512,256]{1,0:T(8,128)(2,1)S(1)} collective-permute-done((bf16[512,256]{1,0:T(8,128)(2,1)S(1)}, bf16[512,256]{1,0:T(8,128)(2,1)S(1)}, u32[]{:S(2)}, u32[]{:S(2)}) %collective-permute-start.12) | collective-permute-done | bytes 262176 | tf_op jit(solution)/shard_map/gather_kv/ppermute | solution.py:185
  73.2 3.8 %collective-permute-start.14 = (bf16[256,256]{1,0:T(8,128)(2,1)S(1)}, bf16[256,256]{1,0:T(8,128)(2,1)S(1)}, u32[]{:S(2)}, u32[]{:S(2)}) collective-permute-start(bf16[256,256]{1,0:T(8,128)(2,1)S(1)} %slice.23), channel_id=1, source_target_pairs={{0,32},{8,40},{16,48},{24,56},{32,64},{40,72},{48,80},{56,88},{64,... | collective-permute-start | bytes 393224 | tf_op jit(solution)/shard_map/gather_kv/ppermute | solution.py:188
  77.2 2.4 %collective-permute-done.14 = bf16[256,256]{1,0:T(8,128)(2,1)S(1)} collective-permute-done((bf16[256,256]{1,0:T(8,128)(2,1)S(1)}, bf16[256,256]{1,0:T(8,128)(2,1)S(1)}, u32[]{:S(2)}, u32[]{:S(2)}) %collective-permute-start.14) | collective-permute-done | bytes 131104 | tf_op jit(solution)/shard_map/gather_kv/ppermute | solution.py:188
  79.6 3.7 %collective-permute-done.15 = bf16[256,256]{1,0:T(8,128)(2,1)S(1)} collective-permute-done((bf16[256,256]{1,0:T(8,128)(2,1)S(1)}, bf16[256,256]{1,0:T(8,128)(2,1)S(1)}, u32[]{:S(2)}, u32[]{:S(2)}) %collective-permute-start.15) | collective-permute-done | bytes 131104 | tf_op jit(solution)/shard_map/gather_kv/ppermute | solution.py:189
  86.1 12.7 %shard_map.93.ctx_ref = bf16[256,512]{1,0:T(8,128)(2,1)S(1)} custom-call(s32[64]{0:T(128)S(1)} %select_reduce_fusion.slot_ref, s32[2]{0:T(128)S(1)} %get-tuple-element.6.span_ref, s32[3]{0:T(128)S(1)} %pad_add_fusion.bounds_ref, bf16[256,512]{1,0:T(8,128)(2,1)S(1)} %shard_map.91.q_ref, bf16[8192,256]{1,0:T(8,128)(2,1)S(1)} %constant_dynamic-update-slice_fusion.kv_ref), custom_call_target="tpu_custom_call" | custom-call | flops 2147483648 | bytes 5242880 | tf_op jit(solution)/shard_map/pallas_call | solution.py:219
  98.8 1.3 shard_map.94
  100.1 25.7 %all_to_all.5 = bf16[8,256,512]{2,1,0:T(8,128)(2,1)S(1)} all-to-all(bf16[8,256,512]{2,1,0:T(8,128)(2,1)S(1)} %shard_map.94), channel_id=1, replica_groups=mesh['ctx'=32,'tp'=8] {'tp'}, dimensions={0} | all-to-all | bytes 4194304 | tf_op jit(solution)/shard_map/scatter_out/all_to_all | solution.py:240
  125.8 1.0 reduce_sum.32
  (75 shorter events, 6.7 us)
Async XLA Ops:
  0.0 59.2 %copy-start.5 = (bf16[256,512]{1,0:T(8,128)(2,1)S(1)}, bf16[256,512]{1,0:T(8,128)(2,1)}, u32[]{:S(2)}) copy-start(bf16[256,512]{1,0:T(8,128)(2,1)} %refs_0_.3) | copy-start | bytes 786436
  0.0 50.5 %copy-start.7 = (s32[64]{0:T(128)S(1)}, s32[64]{0:T(128)}, u32[]{:S(2)}) copy-start(s32[64]{0:T(128)} %param.14) | copy-start | bytes 772
  0.0 43.0 %copy-start.6 = (s32[4]{0:T(128)S(1)}, s32[4]{0:T(128)}, u32[]{:S(2)}) copy-start(s32[4]{0:T(128)} %param.15) | copy-start | bytes 52
  0.0 10.9 %collective-permute-start = (bf16[256,512]{1,0:T(8,128)(2,1)}, bf16[256,512]{1,0:T(8,128)(2,1)S(1)}, u32[]{:S(2)}, u32[]{:S(2)}) collective-permute-start(bf16[256,512]{1,0:T(8,128)(2,1)} %refs_0_.3), channel_id=1, source_target_pairs={{0,7},{1,0},{2,1},{3,2},{4,3},{5,4},{6,5},{7,6},{8,15},{9,8},{10,9... | collective-permute-start | bytes 786440 | tf_op jit(solution)/shard_map/gather_hidden/ppermute | solution.py:159
  3.9 22.8 %collective-permute-start.1 = (bf16[256,512]{1,0:T(8,128)(2,1)}, bf16[256,512]{1,0:T(8,128)(2,1)S(1)}, u32[]{:S(2)}, u32[]{:S(2)}) collective-permute-start(bf16[256,512]{1,0:T(8,128)(2,1)} %refs_0_.3), channel_id=1, source_target_pairs={{0,6},{1,7},{2,0},{3,1},{4,2},{5,3},{6,4},{7,5},{8,14},{9,15},{10,... | collective-permute-start | bytes 786440 | tf_op jit(solution)/shard_map/gather_hidden/ppermute | solution.py:159
  4.7 22.1 %collective-permute-start.2 = (bf16[256,512]{1,0:T(8,128)(2,1)}, bf16[256,512]{1,0:T(8,128)(2,1)S(1)}, u32[]{:S(2)}, u32[]{:S(2)}) collective-permute-start(bf16[256,512]{1,0:T(8,128)(2,1)} %refs_0_.3), channel_id=1, source_target_pairs={{0,5},{1,6},{2,7},{3,0},{4,1},{5,2},{6,3},{7,4},{8,13},{9,14},{10,... | collective-permute-start | bytes 786440 | tf_op jit(solution)/shard_map/gather_hidden/ppermute | solution.py:159
  5.1 21.7 %collective-permute-start.3 = (bf16[256,512]{1,0:T(8,128)(2,1)}, bf16[256,512]{1,0:T(8,128)(2,1)S(1)}, u32[]{:S(2)}, u32[]{:S(2)}) collective-permute-start(bf16[256,512]{1,0:T(8,128)(2,1)} %refs_0_.3), channel_id=1, source_target_pairs={{0,4},{1,5},{2,6},{3,7},{4,0},{5,1},{6,2},{7,3},{8,12},{9,13},{10,... | collective-permute-start | bytes 786440 | tf_op jit(solution)/shard_map/gather_hidden/ppermute | solution.py:159
  7.8 21.9 %collective-permute-start.4 = (bf16[256,512]{1,0:T(8,128)(2,1)}, bf16[256,512]{1,0:T(8,128)(2,1)S(1)}, u32[]{:S(2)}, u32[]{:S(2)}) collective-permute-start(bf16[256,512]{1,0:T(8,128)(2,1)} %refs_0_.3), channel_id=1, source_target_pairs={{0,3},{1,4},{2,5},{3,6},{4,7},{5,0},{6,1},{7,2},{8,11},{9,12},{10,... | collective-permute-start | bytes 786440 | tf_op jit(solution)/shard_map/gather_hidden/ppermute | solution.py:159
  10.9 22.7 %collective-permute-start.5 = (bf16[256,512]{1,0:T(8,128)(2,1)}, bf16[256,512]{1,0:T(8,128)(2,1)S(1)}, u32[]{:S(2)}, u32[]{:S(2)}) collective-permute-start(bf16[256,512]{1,0:T(8,128)(2,1)} %refs_0_.3), channel_id=1, source_target_pairs={{0,2},{1,3},{2,4},{3,5},{4,6},{5,7},{6,0},{7,1},{8,10},{9,11},{10,... | collective-permute-start | bytes 786440 | tf_op jit(solution)/shard_map/gather_hidden/ppermute | solution.py:159
  26.6 8.7 %collective-permute-start.6 = (bf16[256,512]{1,0:T(8,128)(2,1)}, bf16[256,512]{1,0:T(8,128)(2,1)S(1)}, u32[]{:S(2)}, u32[]{:S(2)}) collective-permute-start(bf16[256,512]{1,0:T(8,128)(2,1)} %refs_0_.3), channel_id=1, source_target_pairs={{0,1},{1,2},{2,3},{3,4},{4,5},{5,6},{6,7},{7,0},{8,9},{9,10},{10,1... | collective-permute-start | bytes 786440 | tf_op jit(solution)/shard_map/gather_hidden/ppermute | solution.py:159
  35.3 1.2 copy-start.2
  36.5 1.2 copy-start.3
  40.0 6.6 %collective-permute-start.7 = (bf16[256,256]{1,0:T(8,128)(2,1)S(1)}, bf16[256,256]{1,0:T(8,128)(2,1)S(1)}, u32[]{:S(2)}, u32[]{:S(2)}) collective-permute-start(bf16[256,256]{1,0:T(8,128)(2,1)S(1)} %shard_map.92), channel_id=1, source_target_pairs={{0,16},{8,24},{16,0},{24,8},{32,48},{40,56},{48,32},{56,40},{64,80... | collective-permute-start | bytes 393224 | tf_op jit(solution)/shard_map/gather_kv/ppermute | solution.py:180
  46.6 8.5 %collective-permute-start.8 = (bf16[512,256]{1,0:T(8,128)(2,1)S(1)}, bf16[512,256]{1,0:T(8,128)(2,1)S(1)}, u32[]{:S(2)}, u32[]{:S(2)}) collective-permute-start(bf16[512,256]{1,0:T(8,128)(2,1)S(1)} %pad_maximum_fusion), channel_id=1, source_target_pairs={{0,32},{8,40},{16,48},{24,56},{32,64},{40,72},{48,80},{56,88},{64,... | collective-permute-start | bytes 786440 | tf_op jit(solution)/shard_map/gather_kv/ppermute | solution.py:185
  49.8 9.4 %collective-permute-start.9 = (bf16[512,256]{1,0:T(8,128)(2,1)S(1)}, bf16[512,256]{1,0:T(8,128)(2,1)S(1)}, u32[]{:S(2)}, u32[]{:S(2)}) collective-permute-start(bf16[512,256]{1,0:T(8,128)(2,1)S(1)} %pad_maximum_fusion), channel_id=1, source_target_pairs={{0,224},{8,232},{16,240},{24,248},{32,0},{40,8},{48,16},{56,24},{6... | collective-permute-start | bytes 786440 | tf_op jit(solution)/shard_map/gather_kv/ppermute | solution.py:186
  55.1 8.6 %collective-permute-start.10 = (bf16[512,256]{1,0:T(8,128)(2,1)S(1)}, bf16[512,256]{1,0:T(8,128)(2,1)S(1)}, u32[]{:S(2)}, u32[]{:S(2)}) collective-permute-start(bf16[512,256]{1,0:T(8,128)(2,1)S(1)} %collective-permute-done.8), channel_id=1, source_target_pairs={{0,32},{8,40},{16,48},{24,56},{32,64},{40,72},{48,80},{56,88},{64,... | collective-permute-start | bytes 786440 | tf_op jit(solution)/shard_map/gather_kv/ppermute | solution.py:185
  59.1 7.9 %collective-permute-start.11 = (bf16[512,256]{1,0:T(8,128)(2,1)S(1)}, bf16[512,256]{1,0:T(8,128)(2,1)S(1)}, u32[]{:S(2)}, u32[]{:S(2)}) collective-permute-start(bf16[512,256]{1,0:T(8,128)(2,1)S(1)} %collective-permute-done.9), channel_id=1, source_target_pairs={{0,224},{8,232},{16,240},{24,248},{32,0},{40,8},{48,16},{56,24},{6... | collective-permute-start | bytes 786440 | tf_op jit(solution)/shard_map/gather_kv/ppermute | solution.py:186
  59.2 2.2 %copy-start = (bf16[4096,512]{1,0:T(8,128)(2,1)S(1)}, bf16[4096,512]{1,0:T(8,128)(2,1)}, u32[]{:S(2)}) copy-start(bf16[4096,512]{1,0:T(8,128)(2,1)} %refs_8_.2) | copy-start | bytes 12582916
  62.7 20.6 %collective-permute-start.16 = (bf16[512,256]{1,0:T(8,128)(2,1)S(1)}, bf16[512,256]{1,0:T(8,128)(2,1)S(1)}, u32[]{:S(2)}, u32[]{:S(2)}) collective-permute-start(bf16[512,256]{1,0:T(8,128)(2,1)S(1)} %pad_maximum_fusion), channel_id=1, source_target_pairs={{0,8},{8,0},{16,24},{24,16},{32,40},{40,32},{48,56},{56,48},{64,72... | collective-permute-start | bytes 786440 | tf_op jit(solution)/shard_map/gather_kv/ppermute | solution.py:193
  63.0 20.9 %collective-permute-start.17 = (bf16[512,256]{1,0:T(8,128)(2,1)S(1)}, bf16[512,256]{1,0:T(8,128)(2,1)S(1)}, u32[]{:S(2)}, u32[]{:S(2)}) collective-permute-start(bf16[512,256]{1,0:T(8,128)(2,1)S(1)} %collective-permute-done.8), channel_id=1, source_target_pairs={{0,8},{8,0},{16,24},{24,16},{32,40},{40,32},{48,56},{56,48},{64,72... | collective-permute-start | bytes 786440 | tf_op jit(solution)/shard_map/gather_kv/ppermute | solution.py:193
  63.6 20.4 %collective-permute-start.18 = (bf16[512,256]{1,0:T(8,128)(2,1)S(1)}, bf16[512,256]{1,0:T(8,128)(2,1)S(1)}, u32[]{:S(2)}, u32[]{:S(2)}) collective-permute-start(bf16[512,256]{1,0:T(8,128)(2,1)S(1)} %collective-permute-done.9), channel_id=1, source_target_pairs={{0,8},{8,0},{16,24},{24,16},{32,40},{40,32},{48,56},{56,48},{64,72... | collective-permute-start | bytes 786440 | tf_op jit(solution)/shard_map/gather_kv/ppermute | solution.py:193
  63.7 9.5 %collective-permute-start.12 = (bf16[512,256]{1,0:T(8,128)(2,1)S(1)}, bf16[512,256]{1,0:T(8,128)(2,1)S(1)}, u32[]{:S(2)}, u32[]{:S(2)}) collective-permute-start(bf16[512,256]{1,0:T(8,128)(2,1)S(1)} %collective-permute-done.10), channel_id=1, source_target_pairs={{0,32},{8,40},{16,48},{24,56},{32,64},{40,72},{48,80},{56,88},{64,... | collective-permute-start | bytes 786440 | tf_op jit(solution)/shard_map/gather_kv/ppermute | solution.py:185
  67.1 9.9 %collective-permute-start.13 = (bf16[512,256]{1,0:T(8,128)(2,1)S(1)}, bf16[512,256]{1,0:T(8,128)(2,1)S(1)}, u32[]{:S(2)}, u32[]{:S(2)}) collective-permute-start(bf16[512,256]{1,0:T(8,128)(2,1)S(1)} %collective-permute-done.11), channel_id=1, source_target_pairs={{0,224},{8,232},{16,240},{24,248},{32,0},{40,8},{48,16},{56,24},{6... | collective-permute-start | bytes 786440 | tf_op jit(solution)/shard_map/gather_kv/ppermute | solution.py:186
  73.2 6.3 %collective-permute-start.14 = (bf16[256,256]{1,0:T(8,128)(2,1)S(1)}, bf16[256,256]{1,0:T(8,128)(2,1)S(1)}, u32[]{:S(2)}, u32[]{:S(2)}) collective-permute-start(bf16[256,256]{1,0:T(8,128)(2,1)S(1)} %slice.23), channel_id=1, source_target_pairs={{0,32},{8,40},{16,48},{24,56},{32,64},{40,72},{48,80},{56,88},{64,... | collective-permute-start | bytes 393224 | tf_op jit(solution)/shard_map/gather_kv/ppermute | solution.py:188
  77.0 6.3 %collective-permute-start.15 = (bf16[256,256]{1,0:T(8,128)(2,1)S(1)}, bf16[256,256]{1,0:T(8,128)(2,1)S(1)}, u32[]{:S(2)}, u32[]{:S(2)}) collective-permute-start(bf16[256,256]{1,0:T(8,128)(2,1)S(1)} %slice.24), channel_id=1, source_target_pairs={{0,224},{8,232},{16,240},{24,248},{32,0},{40,8},{48,16},{56,24},{6... | collective-permute-start | bytes 393224 | tf_op jit(solution)/shard_map/gather_kv/ppermute | solution.py:189
  79.6 5.1 %collective-permute-start.19 = (bf16[512,256]{1,0:T(8,128)(2,1)S(1)}, bf16[512,256]{1,0:T(8,128)(2,1)S(1)}, u32[]{:S(2)}, u32[]{:S(2)}) collective-permute-start(bf16[512,256]{1,0:T(8,128)(2,1)S(1)} %collective-permute-done.10), channel_id=1, source_target_pairs={{0,8},{8,0},{16,24},{24,16},{32,40},{40,32},{48,56},{56,48},{64,72... | collective-permute-start | bytes 786440 | tf_op jit(solution)/shard_map/gather_kv/ppermute | solution.py:193
  83.3 1.5 %collective-permute-start.20 = (bf16[512,256]{1,0:T(8,128)(2,1)S(1)}, bf16[512,256]{1,0:T(8,128)(2,1)S(1)}, u32[]{:S(2)}, u32[]{:S(2)}) collective-permute-start(bf16[512,256]{1,0:T(8,128)(2,1)S(1)} %collective-permute-done.11), channel_id=1, source_target_pairs={{0,8},{8,0},{16,24},{24,16},{32,40},{40,32},{48,56},{56,48},{64,72... | collective-permute-start | bytes 786440 | tf_op jit(solution)/shard_map/gather_kv/ppermute | solution.py:193
  83.3 1.9 %collective-permute-start.21 = (bf16[512,256]{1,0:T(8,128)(2,1)S(1)}, bf16[512,256]{1,0:T(8,128)(2,1)S(1)}, u32[]{:S(2)}, u32[]{:S(2)}) collective-permute-start(bf16[512,256]{1,0:T(8,128)(2,1)S(1)} %collective-permute-done.12), channel_id=1, source_target_pairs={{0,8},{8,0},{16,24},{24,16},{32,40},{40,32},{48,56},{56,48},{64,72... | collective-permute-start | bytes 786440 | tf_op jit(solution)/shard_map/gather_kv/ppermute | solution.py:193
  83.9 1.6 %collective-permute-start.22 = (bf16[512,256]{1,0:T(8,128)(2,1)S(1)}, bf16[512,256]{1,0:T(8,128)(2,1)S(1)}, u32[]{:S(2)}, u32[]{:S(2)}) collective-permute-start(bf16[512,256]{1,0:T(8,128)(2,1)S(1)} %collective-permute-done.13), channel_id=1, source_target_pairs={{0,8},{8,0},{16,24},{24,16},{32,40},{40,32},{48,56},{56,48},{64,72... | collective-permute-start | bytes 786440 | tf_op jit(solution)/shard_map/gather_kv/ppermute | solution.py:193
  84.1 1.7 %collective-permute-start.23 = (bf16[256,256]{1,0:T(8,128)(2,1)S(1)}, bf16[256,256]{1,0:T(8,128)(2,1)S(1)}, u32[]{:S(2)}, u32[]{:S(2)}) collective-permute-start(bf16[256,256]{1,0:T(8,128)(2,1)S(1)} %collective-permute-done.14), channel_id=1, source_target_pairs={{0,8},{8,0},{16,24},{24,16},{32,40},{40,32},{48,56},{56,48},{64,72... | collective-permute-start | bytes 393224 | tf_op jit(solution)/shard_map/gather_kv/ppermute | solution.py:193
  84.7 1.4 %collective-permute-start.24 = (bf16[256,256]{1,0:T(8,128)(2,1)S(1)}, bf16[256,256]{1,0:T(8,128)(2,1)S(1)}, u32[]{:S(2)}, u32[]{:S(2)}) collective-permute-start(bf16[256,256]{1,0:T(8,128)(2,1)S(1)} %collective-permute-done.15), channel_id=1, source_target_pairs={{0,8},{8,0},{16,24},{24,16},{32,40},{40,32},{48,56},{56,48},{64,72... | collective-permute-start | bytes 393224 | tf_op jit(solution)/shard_map/gather_kv/ppermute | solution.py:193
  85.6 13.2 %copy-start.1 = (bf16[512,4096]{1,0:T(8,128)(2,1)S(1)}, bf16[512,4096]{1,0:T(8,128)(2,1)}, u32[]{:S(2)}) copy-start(bf16[512,4096]{1,0:T(8,128)(2,1)} %w_ref.1) | copy-start | bytes 12582916
  (1 other events, 0.9 us)
